TPU v7x, 256 devices: a whole 4x4x8 slice. The times are simulated.
256 devices in a mesh: seq: 64 (over y, z, x_lo), tp: 4 (over x_hi, core).
Axes of the slice: x: 4 (x_hi: 2, x_lo: 2; x = x_hi * 2 + x_lo), y: 4, z: 8, core: 2. Of those that a mesh axis runs over, the one named last changes fastest.
Arguments:
- token_ids: int32 [8192], P('seq'), may hold values from 0 to 511
- embedding: bfloat16 [512, 8192], P(None, 'tp'), may hold values from -800 to 800
- norm_gain: float32 [8192], P('tp'), may hold values from 0.1 to 1.9
- projection: bfloat16 [8192, 3, 8192], P('tp', None, 'seq'), may hold values from -0.0625 to 0.0625
- short_filter: float32 [3, 3, 8192], replicated, may hold values from -3.5 to 3.5
- residues: float32 [8192, 16], replicated, may hold values from -1.8 to 1.8
- decay_rates: float32 [8192, 16], replicated, may hold values from 6.1035156e-05 to 0.04
Outputs:
- hyena_out: bfloat16 [8192, 8192], P(('seq', 'tp'))
Inputs may be any that keep to these rules, and one draw needn't show every extreme that they name: `token_ids`: ids of a 512-entry vocabulary.
All inputs are finite; a program needn't handle non-finite values.
Results may differ from a plain program's by a relative error of at most 0.0079.
Values may be sent and summed in bfloat16 or wider, within the bound.
A program may use at most 128 MiB of HBM per device.

v0:
```python
import jax
import jax.numpy as jnp
from jax import lax
from jax.sharding import PartitionSpec as P


def from_behind(value, axis, by):
    peers = lax.axis_size(axis)
    pairs = [(i, i + by) for i in range(peers) if 0 <= i + by < peers]
    return lax.ppermute(value, axis, pairs)


def carried_in(part, axis, combine, identity):
    place = lax.axis_index(axis)
    gathered = jax.tree.map(lambda a: lax.all_gather(a, axis), part)
    state = jax.tree.map(lambda a, e: jnp.zeros_like(a) + jnp.asarray(e, a.dtype), part, identity)

    def one(turn, state):
        return combine(
            state, jax.tree.map(lambda a: lax.dynamic_index_in_dim(a, turn, 0, False), gathered)
        )

    return lax.fori_loop(0, place, one, state)


def compose(earlier, later):
    return (earlier[0] * later[0], later[0] * earlier[1] + later[1])


def row_states(blocked, rate_rows):
    span_len = blocked.shape[1]
    states = jnp.zeros((blocked.shape[0],) + rate_rows.shape, jnp.float32)
    for within in range(span_len):
        factor = jnp.exp(-rate_rows * (span_len - 1.0 - within))
        states = states + factor[None, :, :] * blocked[:, within, None, :]
    return states


def row_end(states, rate_rows, span_len):
    blocks = states.shape[0]
    behind = (span_len * (blocks - 1 - jnp.arange(blocks))).astype(jnp.float32)
    return jnp.sum(jnp.exp(-rate_rows[None, :, :] * behind[:, None, None]) * states, axis=0)


def row_modes(blocked, states, rate_rows, mode_rows, carry_in):
    blocks, span_len, channels = blocked.shape
    step_decay = jnp.broadcast_to(jnp.exp(-rate_rows * span_len)[None, :, :], states.shape)
    inclusive = lax.associative_scan(compose, (step_decay, states), axis=0)[1]
    ahead = (span_len * jnp.arange(blocks)).astype(jnp.float32)
    exclusive = jnp.concatenate([jnp.zeros_like(states[:1]), inclusive[:-1]], axis=0)
    exclusive = (
        exclusive + jnp.exp(-rate_rows[None, :, :] * ahead[:, None, None]) * carry_in[None, :, :]
    )
    within = jnp.arange(span_len, dtype=jnp.float32)
    across = jnp.zeros(blocked.shape, jnp.float32)
    kernel = jnp.zeros((span_len, channels), jnp.float32)
    for mode in range(rate_rows.shape[0]):
        lead = mode_rows[mode][None, :] * jnp.exp(
            -rate_rows[mode][None, :] * (within + 1.0)[:, None]
        )
        across = across + exclusive[:, mode, None, :] * lead[None, :, :]
        kernel = kernel + mode_rows[mode][None, :] * jnp.exp(
            -rate_rows[mode][None, :] * within[:, None]
        )
    padded = jnp.pad(blocked, ((0, 0), (span_len - 1, 0), (0, 0)))
    inside = jnp.zeros(blocked.shape, jnp.float32)
    for lag in range(span_len):
        inside = (
            inside
            + kernel[lag][None, None, :] * padded[:, span_len - 1 - lag : 2 * span_len - 1 - lag, :]
        )
    return (inside + across).reshape(blocks * span_len, channels)


def pick_group(values, seq_count, tp_count, unit_width, tp_place):
    shaped = values.reshape((seq_count, tp_count, unit_width) + values.shape[1:])
    chosen = lax.dynamic_index_in_dim(shaped, tp_place, axis=1, keepdims=False)
    return chosen.reshape((seq_count * unit_width,) + values.shape[1:])


def on_device(token_ids, embedding, norm_gain, projection, short_filter, residues, decay_rates):
    seq_count = lax.axis_size("seq")
    tp_count = lax.axis_size("tp")
    tp_place = lax.axis_index("tp")
    vocab_size = embedding.shape[0]
    model_width = short_filter.shape[2]
    features = embedding.astype(jnp.float32)
    energy = lax.psum(jnp.sum(features * features, axis=1), "tp")
    normed = (
        features * lax.rsqrt(energy / model_width + 1e-05)[:, None] * norm_gain[None, :]
    ).astype(jnp.bfloat16)
    block_width = projection.shape[2]
    unit_width = block_width // tp_count
    lookup_table = lax.psum_scatter(
        jnp.einsum("dsc,vd->csv", projection, normed, preferred_element_type=jnp.float32),
        "tp",
        scatter_dimension=0,
        tiled=True,
    ).astype(jnp.bfloat16)
    mode_all = residues * jnp.sqrt(-jnp.expm1(-2.0 * decay_rates))
    taps_all = jnp.transpose(short_filter, (2, 0, 1))
    taps_count = short_filter.shape[1]
    vocab_index = jnp.arange(vocab_size, dtype=jnp.int32)
    tokens = token_ids.shape[0]
    onehot = (token_ids[:, None] == vocab_index[None, :]).astype(jnp.bfloat16)
    streams = jnp.einsum(
        "csv,lv->slc",
        lax.all_gather(lookup_table, "seq", axis=0, tiled=True),
        onehot,
        preferred_element_type=jnp.float32,
    ).astype(jnp.bfloat16)
    streams = lax.optimization_barrier(streams)
    rate_rows = jnp.transpose(pick_group(decay_rates, seq_count, tp_count, unit_width, tp_place))
    mode_rows = jnp.transpose(pick_group(mode_all, seq_count, tp_count, unit_width, tp_place))
    taps_own = pick_group(taps_all, seq_count, tp_count, unit_width, tp_place)
    rim_rows = from_behind(streams[:, tokens - (taps_count - 1) :, :], "seq", 1)
    extended = jnp.concatenate([rim_rows, streams], axis=1)
    filtered = jnp.zeros(streams.shape, jnp.float32)
    for tap_index in range(taps_count):
        lag_start = taps_count - 1 - tap_index
        window = lax.slice_in_dim(extended, lag_start, lag_start + tokens, axis=1).astype(
            jnp.float32
        )
        filtered = filtered + jnp.transpose(taps_own[:, :, tap_index])[:, None, :] * window
    gated_in = lax.optimization_barrier((filtered[1] * filtered[2]).astype(jnp.bfloat16)).astype(
        jnp.float32
    )
    span_len = 16
    blocked = gated_in.reshape(tokens // span_len, span_len, gated_in.shape[1])
    states = row_states(blocked, rate_rows)
    end_state = row_end(states, rate_rows, span_len)
    decay_block = jnp.exp(-rate_rows * tokens)
    carry_in = carried_in(
        (decay_block, end_state),
        "seq",
        compose,
        (jnp.ones_like(decay_block), jnp.zeros_like(end_state)),
    )[1]
    long_out = row_modes(blocked, states, rate_rows, mode_rows, carry_in)
    mixed_out = jnp.transpose((filtered[0] * long_out).astype(jnp.bfloat16))
    return lax.all_to_all(mixed_out, "seq", split_axis=0, concat_axis=1, tiled=True)


def solution(mesh):
    return jax.shard_map(
        on_device,
        mesh=mesh,
        in_specs=(P("seq"), P(None, "tp"), P("tp"), P("tp", None, "seq"), P(), P(), P()),
        out_specs=P(("seq", "tp"), None),
        check_vma=False,
    )
```

profile of v0, /device:TPU:4, one launch (start us, length us, event | category | flops | bytes accessed | tf_op | source)
XLA Modules:
  0.0 1090.2 jit_solution(2338216775836615640)
XLA Ops:
  6.5 2.2 fusion
  8.7 7.2 psum.7
  15.9 2.9 fusion.10
  19.3 30.5 %all-reduce.10 = bf16[128,3,512]{2,1,0:T(4,128)(2,1)S(1)} all-reduce(f32[128,3,512]{2,1,0:T(4,128)S(1)} %copy.19), channel_id=4, replica_groups=mesh['seq'=64,'tp'=4] {'tp'}, use_global_device_ids=true, to_apply=%region_2.0.clone | all-reduce | flops 196608 | bytes 1179648
  51.9 2.5 reshape.850
  54.7 2.5 reshape.848
  57.1 5.5 dynamic-slice_reduce_fusion
  62.9 1.2 multiply_exponential_fusion
  65.0 0.9 dynamic-slice_reduce_fusion.2
  67.3 296.8 %all-gather.6.cloned.1.call-done = bf16[2048,3,512]{2,0,1:T(8,128)(2,1)} async-done(((bf16[32,3,512]{2,0,1:T(8,128)(2,1)}), bf16[2048,3,512]{2,0,1:T(8,128)(2,1)}) %all-gather.6.cloned.1.call-update) | async-done | bytes 6291472 | tf_op jit(solution)/shard_map/all_gather | solution.py:108
  364.1 5.0 fusion.3
  369.1 1.7 collective-permute-start
  370.9 1.5 collective-permute-done
  372.3 1.2 multiply_add_fusion
  373.5 1.6 copy-done.2
  375.3 1.0 fusion.59
  376.9 2.1 multiply_reduce_fusion
  380.5 0.7 fusion.60
  381.3 1.0 exponential_multiply_fusion.6
  382.3 1.1 exponential_multiply_fusion.15
  385.1 1.0 pad.28
  386.2 0.9 add.370
  387.1 1.0 fusion.48
  388.1 2.3 pad.40
  390.4 2.0 pad.175
  392.4 1.3 slice_add_fusion.3
  393.7 283.4 %all-gather.8.cloned.1.call-done = f32[1024,2048]{1,0:T(8,128)} async-done(((f32[16,2048]{1,0:T(8,128)}), f32[1024,2048]{1,0:T(8,128)}) %all-gather.8.cloned.1.call-update) | async-done | bytes 8388624 | tf_op jit(solution)/shard_map/all_gather | solution.py:15
  677.2 312.7 %all-gather.10.cloned.1.call-done = f32[1024,2048]{1,0:T(8,128)} async-done(((f32[16,2048]{1,0:T(8,128)}), f32[1024,2048]{1,0:T(8,128)}) %all-gather.10.cloned.1.call-update) | async-done | bytes 8388624 | tf_op jit(solution)/shard_map/all_gather | solution.py:15
  992.3 3.4 fusion.29
  995.7 1.3 fusion.46
  997.3 85.5 %all_to_all.19 = bf16[64,32,128]{2,1,0:T(8,128)(2,1)S(1)} all-to-all(bf16[64,32,128]{2,1,0:T(8,128)(2,1)S(1)} %bitcast.274), channel_id=1, replica_groups=mesh['seq'=64,'tp'=4] {'seq'}, dimensions={0} | all-to-all | bytes 1048576 | tf_op jit(solution)/shard_map/all_to_all | solution.py:141
  1082.8 0.8 copy_bitcast_fusion
  (183 shorter events, 10.6 us)
Async XLA Ops:
  6.5 9.4 copy-start
  6.5 357.6 %all-gather.6.cloned.1.call-start = ((), (), s32[]{:S(2)}) async-start(), calls=%async_computation.1 | async-start | bytes 6389760 | tf_op jit(solution)/shard_map/all_gather | solution.py:108
  18.8 31.0 %copy-start.54 = (u32[256]{0:T(256)S(1)}, u32[256]{0:T(256)}, u32[]{:S(2)}) copy-start(u32[256]{0:T(256)} %constant.104) | copy-start | bytes 3076
  18.8 33.1 %copy-start.3 = (f32[8192,16]{0,1:T(8,128)S(1)}, f32[8192,16]{0,1:T(8,128)}, u32[]{:S(2)}) copy-start(f32[8192,16]{0,1:T(8,128)} %param.15) | copy-start | bytes 1572868
  18.8 35.5 %copy-start.7 = (f32[8192,16]{0,1:T(8,128)S(1)}, f32[8192,16]{0,1:T(8,128)}, u32[]{:S(2)}) copy-start(f32[8192,16]{0,1:T(8,128)} %param.14) | copy-start | bytes 1572868
  51.8 625.3 %all-gather.8.cloned.1.call-start = ((), (), s32[]{:S(2)}) async-start(), calls=%async_computation.2 | async-start | bytes 8519680 | tf_op jit(solution)/shard_map/all_gather | solution.py:15
  57.1 7.2 copy-start.34
  62.6 301.5 %copy-start.52 = (s32[128]{0:T(128)S(1)}, s32[128]{0:T(128)}, u32[]{:S(2)}) copy-start(s32[128]{0:T(128)} %param.9) | copy-start | bytes 1540
  64.1 312.8 %copy-start.4 = (f32[16,2048]{1,0:T(8,128)}, f32[16,2048]{1,0:T(8,128)S(1)}, u32[]{:S(2)}) copy-start(f32[16,2048]{1,0:T(8,128)S(1)} %get-tuple-element.165) | copy-start | bytes 393220
  64.1 320.1 %copy-start.6 = (f32[16,2048]{1,0:T(8,128)}, f32[16,2048]{1,0:T(8,128)S(1)}, u32[]{:S(2)}) copy-start(f32[16,2048]{1,0:T(8,128)S(1)} %get-tuple-element.163) | copy-start | bytes 393220
  64.1 925.8 %all-gather.10.cloned.1.call-start = ((), (), s32[]{:S(2)}) async-start(), calls=%async_computation.3 | async-start | bytes 8519680 | tf_op jit(solution)/shard_map/all_gather | solution.py:15
  364.1 6.7 copy-start.37
  364.1 8.2 copy-start.35
  364.1 8.2 copy-start.36
  369.1 3.2 collective-permute-start
  386.1 1.9 copy-start.8
  392.4 597.8 %copy-start.5 = (f32[16,2048]{1,0:T(8,128)S(1)}, f32[16,2048]{1,0:T(8,128)}, u32[]{:S(2)}) copy-start(f32[16,2048]{1,0:T(8,128)} %copy-done.4) | copy-start | bytes 393220
  392.4 597.8 %copy-start.53 = (f32[8]{0:T(128)S(1)}, f32[8]{0:T(128)}, u32[]{:S(2)}) copy-start(f32[8]{0:T(128)} %multiply_convert_fusion.1) | copy-start | bytes 100
  990.2 1.8 copy-start.18
  990.2 1.8 copy-start.19
  990.2 1.8 copy-start.20
  990.2 1.8 copy-start.21
  990.2 1.8 copy-start.22
  990.2 1.8 copy-start.23
  990.3 1.8 copy-start.24
  990.3 1.8 copy-start.25
  990.3 1.8 copy-start.26
  990.3 1.8 copy-start.27
  990.3 1.8 copy-start.28
  990.3 1.8 copy-start.29
  990.3 1.8 copy-start.30
  992.3 91.3 %copy-start.1 = (bf16[2048,3,128]{2,0,1:T(8,128)(2,1)S(1)}, bf16[2048,3,128]{2,0,1:T(8,128)(2,1)}, u32[]{:S(2)}) copy-start(bf16[2048,3,128]{2,0,1:T(8,128)(2,1)} %param.12) | copy-start | bytes 4718596
  (27 other events, 47.1 us)
Sparse Core Ops, SparseCore 0:
  52.0 312.1 all-gather.5
  365.9 311.2 all-gather.7
  679.0 310.9 all-gather.9
where the time goes:
time: 1090 us
  waiting for transfers between devices  894 us (82%)
  blocking collectives  123 us (11%)
  local copies, waits for them, and re-layouts  27.9 us (3%)
  other arithmetic  19.5 us (2%)
  between operations  15 us (1%)
    all_gather x2, waiting for transfers between devices, carried_in(): gathered = jax.tree.map(lambda a: lax.all_gather(a, axis), part)  596 us
    all_gather x1, waiting for transfers between devices, on_device(): lax.all_gather(lookup_table, 'seq', axis=0, tiled=True)  297 us
    all_to_all x1, blocking collectives, on_device(): lax.all_to_all(mixed_out, 'seq', split_axis=0, concat_axis=1, tiled=True)  85.5 us
    unnamed x1, blocking collectives  30.5 us
  transfers between devices with their start and end apart: 4, of which 4 were waited for; matrix products, arithmetic and copies ran while one was open for 4% of the time, Pallas kernels for 0%

commit v1 on v0

v1 whole, which is shorter than its diff:
```python
import functools

import jax
import jax.numpy as jnp
from jax import lax
from jax.experimental import pallas as pl
from jax.experimental.pallas import tpu as pltpu
from jax.sharding import PartitionSpec as P

MESH = pl.DeviceIdType.MESH
F32 = jnp.float32
BF16 = jnp.bfloat16
LANES = 128
CHANNELS = 32
MODES = 16
STREAMS = 3
TAPS = 3
VOCAB = 512
HALF = 256
ORDER = (1, 2, 0)


def split(x):
    hi = x.astype(BF16)
    return hi, (x - hi.astype(F32)).astype(BF16)


def quad_operands(x):
    hi = x.astype(BF16).astype(F32)
    lo = x - hi
    lane = lax.broadcasted_iota(jnp.int32, x.shape, 1)
    low = lane < 64
    first = jnp.where(low, hi, pltpu.roll(lo, 64, 1))
    second = jnp.where(low, pltpu.roll(hi, 64, 1), lo)
    hi = hi.astype(BF16)
    return (
        jnp.concatenate([first.astype(BF16), hi], axis=1),
        jnp.concatenate([second.astype(BF16), hi], axis=1),
    )


def kernel(
    model_width,
    seq_count,
    emb_hbm,
    gain_hbm,
    proj_hbm,
    ids_hbm,
    filt_hbm,
    res_hbm,
    rate_hbm,
    obuf,
    emb,
    gain,
    proj,
    ids,
    filt,
    res,
    rate,
    wproj,
    part,
    recv1,
    own,
    send2,
    recv2,
    en_part,
    en_own,
    en_recv1,
    en_sum,
    en_recv2,
    tblkv,
    tblq,
    onehot,
    taps,
    weights,
    lquad,
    colw,
    step_rate,
    gated,
    qfilt,
    yintra,
    ends,
    carries,
    ybuf,
    load_sem,
    id_send,
    id_recv,
    s1_send,
    s1_recv,
    s2_send,
    s2_recv,
    e_send,
    e_recv,
):
    seq = lax.axis_index("seq")
    tp = lax.axis_index("tp")
    core = lax.rem(tp, 2)
    far = tp // 2
    sibling = tp + 1 - 2 * core
    across_tp = lax.rem(tp + 2, 4)

    barrier = pltpu.get_barrier_semaphore()
    for peer in (sibling, across_tp):
        pl.semaphore_signal(barrier, inc=1, device_id={"seq": seq, "tp": peer}, device_id_type=MESH)

    def greet(n, _):
        peer = lax.rem(seq + n, seq_count)
        pl.semaphore_signal(barrier, inc=1, device_id={"seq": peer, "tp": tp}, device_id_type=MESH)
        return 0

    lax.fori_loop(1, seq_count, greet, 0)

    rows = emb_hbm.shape[0] // 4
    chan0 = pl.multiple_of(seq * LANES, LANES)
    loads = {}

    def load(name, slot, src, dst):
        loads[name] = pltpu.make_async_copy(src, dst, load_sem.at[slot])
        loads[name].start()

    load("gain", 1, gain_hbm, gain)
    load("proj1", 2, proj_hbm.at[1], proj.at[1])
    for r in range(4):
        load(f"emb{r}", 3 + r, emb_hbm.at[pl.ds(r * rows, rows), :], emb.at[pl.ds(r * rows, rows), :])
    load("ids", 0, ids_hbm, ids.at[seq])
    load("proj2", 7, proj_hbm.at[2], proj.at[2])
    load("proj0", 8, proj_hbm.at[0], proj.at[0])
    load("rate", 9, rate_hbm.at[:, pl.ds(chan0, LANES)], rate)
    load("res", 10, res_hbm.at[:, pl.ds(chan0, LANES)], res)
    load("filt", 11, filt_hbm.at[:, :, pl.ds(chan0, LANES)], filt)

    def ids_copy(n):
        return pltpu.make_async_remote_copy(
            src_ref=ids.at[seq], dst_ref=ids.at[seq],
            send_sem=id_send.at[n], recv_sem=id_recv.at[n],
            device_id={"seq": lax.rem(seq + n, seq_count), "tp": tp}, device_id_type=MESH,
        )

    def send_ids(n, _):
        ids_copy(n).start()
        return 0

    def gained(s):
        loads[f"proj{s}"].wait()

        def one(k, _):
            start = pl.multiple_of(k * LANES, LANES)
            row = gain[pl.ds(k, 1), :]
            column = jnp.transpose(jnp.broadcast_to(row, (LANES, LANES)))
            hi, lo = split(proj[s, pl.ds(start, LANES), :].astype(F32) * column)
            wproj[s, pl.ds(start, LANES), :] = jnp.concatenate([hi, lo], axis=1)
            return 0

        lax.fori_loop(0, proj.shape[1] // LANES, one, 0, unroll=2)

    def project(s, first):
        for r in range(4):
            if first:
                loads[f"emb{r}"].wait()
            block = emb[pl.ds(r * rows, rows), :]
            both = jnp.dot(block, wproj[s], preferred_element_type=F32)
            turned = jnp.transpose(both[:, :LANES] + both[:, LANES:])
            for q in range(4):
                piece = turned[q * CHANNELS:(q + 1) * CHANNELS, :]
                part[s, q % 2, q // 2, :, r * rows:(r + 1) * rows] = piece

    def send_sibling(s):
        copy = pltpu.make_async_remote_copy(
            src_ref=part.at[s, 1 - core], dst_ref=recv1.at[s],
            send_sem=s1_send.at[s], recv_sem=s1_recv.at[s],
            device_id={"seq": seq, "tp": sibling}, device_id_type=MESH,
        )
        copy.start()
        return copy

    def send_across(s, copy):
        copy.wait_recv()
        send2[s] = part[s, core, 1 - far] + recv1[s, 1 - far]
        after = pltpu.make_async_remote_copy(
            src_ref=send2.at[s], dst_ref=recv2.at[s],
            send_sem=s2_send.at[s], recv_sem=s2_recv.at[s],
            device_id={"seq": seq, "tp": across_tp}, device_id_type=MESH,
        )
        after.start()
        own[s] = part[s, core, far] + recv1[s, far]
        return after

    def energies():
        for r in range(4):
            block = emb[pl.ds(r * rows, rows), :]
            total = jnp.zeros((rows, LANES), F32)
            for k in range(emb.shape[1] // LANES):
                piece = block[:, k * LANES:(k + 1) * LANES].astype(F32)
                total = total + piece * piece
            en_part[pl.ds(r, 1), :] = jnp.sum(jnp.transpose(total), axis=0, keepdims=True)

    def send_energy(step, src, dst, peer):
        copy = pltpu.make_async_remote_copy(
            src_ref=src, dst_ref=dst, send_sem=e_send.at[step], recv_sem=e_recv.at[step],
            device_id={"seq": seq, "tp": peer}, device_id_type=MESH,
        )
        copy.start()
        return copy

    loads["gain"].wait()
    gained(1)
    project(1, True)
    gained(2)
    project(2, False)
    loads["ids"].wait()

    pl.semaphore_wait(barrier, seq_count + 1)
    lax.fori_loop(1, seq_count, send_ids, 0)
    sib = {1: send_sibling(1), 2: send_sibling(2)}
    energies()
    energy1 = send_energy(0, en_part, en_recv1, sibling)
    cross = {1: send_across(1, sib[1]), 2: send_across(2, sib[2])}
    gained(0)
    project(0, False)
    sib[0] = send_sibling(0)
    energy1.wait_recv()
    en_sum[...] = en_part[...] + en_recv1[...]
    energy2 = send_energy(1, en_sum, en_recv2, across_tp)
    cross[0] = send_across(0, sib[0])

    loads["rate"].wait()
    loads["res"].wait()
    loads["filt"].wait()
    turn = lax.rem(LANES - tp * CHANNELS, LANES)
    rates = pltpu.roll(rate[...], turn, 1)
    twice = 2.0 * rates
    series = twice * (
        1.0 - twice / 2 * (1.0 - twice / 3 * (1.0 - twice / 4 * (1.0 - twice / 5 * (1.0 - twice / 6))))
    )
    lost = jnp.where(twice < 0.125, series, 1.0 - jnp.exp(-twice))
    mode = pltpu.roll(res[...], turn, 1) * jnp.sqrt(lost)
    lane16 = lax.broadcasted_iota(jnp.int32, (MODES, LANES), 1).astype(F32)
    lquad[...] = jnp.zeros(lquad.shape, BF16)
    for c in range(CHANNELS):
        rate_c = jnp.broadcast_to(rates[:, c:c + 1], (MODES, LANES))
        mode_c = jnp.broadcast_to(mode[:, c:c + 1], (MODES, LANES))
        hi, lo = split(mode_c * jnp.exp(-rate_c * (lane16 + 1.0)))
        colw[pl.ds(c * MODES, MODES), :] = rate_c
        quad, at = c // 4, c % 4
        cols = pl.ds(at * LANES, LANES)
        lquad[quad, pl.ds(at * MODES, MODES), cols] = hi
        lquad[quad, pl.ds(64 + at * MODES, MODES), cols] = hi
        lquad[quad, pl.ds(128 + 64 * (quad % 2) + at * MODES, MODES), cols] = lo
    row_at = lax.broadcasted_iota(jnp.int32, (LANES, LANES), 0)
    lane_at = lax.broadcasted_iota(jnp.int32, (LANES, LANES), 1)
    behind = (LANES - 1 - row_at).astype(F32)
    keep = lane_at >= row_at

    def operators(g, _):
        start = pl.multiple_of(g * LANES, LANES)
        rate_row = jnp.transpose(colw[pl.ds(start, LANES), :])
        step_rate[g] = rate_row[:8, :] * LANES
        decays = jnp.exp(-rate_row * behind)
        e_hi, e_lo = split(decays)
        grown = quad_operands(jnp.exp(rate_row * (row_at + 1).astype(F32)))
        for half in range(2):
            kernels = jnp.dot(grown[half], lquad[g * 2 + half], preferred_element_type=F32)
            for at in range(4):
                inner = jnp.where(keep, kernels[:, at * LANES:(at + 1) * LANES], 0.0)
                t_hi, t_lo = split(inner)
                c_in = half * 4 + at
                mine = (lane_at >= c_in * MODES) & (lane_at < (c_in + 1) * MODES)
                zero = jnp.zeros((LANES, LANES), F32)
                m_hi = jnp.where(mine, e_hi.astype(F32), zero).astype(BF16)
                m_lo = jnp.where(mine, e_lo.astype(F32), zero).astype(BF16)
                c = g * 8 + c_in
                weights[c, pl.ds(0, LANES), :] = jnp.concatenate([t_hi, m_hi], axis=1)
                weights[c, pl.ds(LANES, LANES), :] = jnp.concatenate([t_lo, m_lo], axis=1)
        return 0

    lax.fori_loop(0, 4, operators, 0)

    for s in range(STREAMS):
        moved = pltpu.roll(filt[s], turn, 1)
        columns = jnp.transpose(jnp.concatenate([moved, jnp.zeros((LANES - TAPS, LANES), F32)], axis=0))
        for j in range(TAPS):
            taps[s * TAPS + j] = jnp.broadcast_to(columns[:CHANNELS, j:j + 1], (CHANNELS, LANES))

    row_of = lax.broadcasted_iota(jnp.int32, (HALF, LANES), 0)

    def mark(slot):
        low = jnp.broadcast_to(ids[slot] & (HALF - 1), (HALF, LANES))
        onehot[slot] = jnp.where(row_of == low, 1.0, 0.0).astype(BF16)

    def arrive(n, _):
        ids_copy(n).wait_recv()
        mark(lax.rem(seq + seq_count - n, seq_count))
        return 0

    mark(seq)
    lax.fori_loop(1, seq_count, arrive, 0)

    energy2.wait_recv()
    scale = lax.rsqrt((en_sum[...] + en_recv2[...]) / model_width + 1e-05)

    def tabulate(s, place, table):
        cross[s].wait_recv()
        height = table.shape[0] // 2
        for q in range(4):
            lanes = pl.ds(q * LANES, LANES)
            value = (own[s, :, lanes] + recv2[s, :, lanes]) * scale[q:q + 1, :]
            table[pl.ds((q // 2) * height + place * CHANNELS, CHANNELS), pl.ds((q % 2) * LANES, LANES)] = value.astype(BF16)

    def filter_streams(table, streams, unroll, emit):
        height = table.shape[0] // 2
        lane = lax.broadcasted_iota(jnp.int32, (height, LANES), 1)
        first_lane = lane < 1
        first_two = lane < 2

        def pair(i, carry):
            before1, before2 = carry
            hot = jnp.concatenate([onehot[2 * i], onehot[2 * i + 1]], axis=1)
            both = jnp.dot(table[...], hot, preferred_element_type=F32)
            for u in range(2):
                j = 2 * i + u
                upper = jnp.broadcast_to(ids[j], (height, LANES)) >= HALF
                lanes = slice(u * LANES, (u + 1) * LANES)
                now = jnp.where(upper, both[height:, lanes], both[:height, lanes])
                one, two = pltpu.roll(now, 1, 1), pltpu.roll(now, 2, 1)
                back1 = jnp.where(first_lane, before1, one)
                back2 = jnp.where(first_two, before2, two)
                before1, before2 = one, two
                filtered = []
                for place, s in enumerate(streams):
                    mine = slice(place * CHANNELS, (place + 1) * CHANNELS)
                    filtered.append(
                        taps[s * TAPS] * now[mine] + taps[s * TAPS + 1] * back1[mine] + taps[s * TAPS + 2] * back2[mine]
                    )
                emit(pl.ds(pl.multiple_of(j * CHANNELS, CHANNELS), CHANNELS), *filtered)
            return before1, before2

        nothing = jnp.zeros((height, LANES), F32)
        lax.fori_loop(0, seq_count // 2, pair, (nothing, nothing), unroll=unroll)

    def emit_gated(at, k, v):
        gated[at, :] = (k * v).astype(BF16).astype(F32)

    def emit_query(at, q):
        qfilt[at, :] = q

    tabulate(1, 0, tblkv)
    tabulate(2, 1, tblkv)
    filter_streams(tblkv, (1, 2), 8, emit_gated)
    tabulate(0, 0, tblq)
    filter_streams(tblq, (0,), 8, emit_query)

    def inside(g, _):
        total = jnp.zeros((seq_count, LANES), F32)
        for at in range(8):
            c = g * 8 + at
            x = gated[pl.ds(c, seq_count, stride=CHANNELS), :].astype(BF16)
            result = jnp.dot(jnp.concatenate([x, x], axis=1), weights[c], preferred_element_type=F32)
            yintra[c] = result[:, :LANES]
            total = total + result[:, LANES:]
        ends[g] = total
        return 0

    lax.fori_loop(0, 4, inside, 0)

    sub = lax.broadcasted_iota(jnp.int32, (8, LANES), 0)
    for g in range(4):
        rate_row = step_rate[g]
        own_decay = jnp.exp(-rate_row * sub.astype(F32))
        eighth = jnp.exp(-rate_row * 8.0)
        factors = [(d, jnp.where(sub >= d, jnp.exp(-rate_row * float(d)), 0.0)) for d in (1, 2, 4)]
        entering = jnp.zeros((8, LANES), F32)
        for v in range(seq_count // 8):
            span = ends[g, pl.ds(v * 8, 8), :]
            for d, factor in factors:
                span = span + factor * pltpu.roll(span, d, 0)
            shifted = jnp.where(sub >= 1, pltpu.roll(span, 1, 0), 0.0)
            carries[g, pl.ds(v * 8, 8), :] = shifted + own_decay * entering
            entering = jnp.broadcast_to(span[7:8, :], (8, LANES)) + eighth * entering

    def across(g, _):
        operands = quad_operands(carries[g])
        for half in range(2):
            result = jnp.dot(operands[half], lquad[g * 2 + half], preferred_element_type=F32)
            for at in range(4):
                c = g * 8 + half * 4 + at
                ybuf[pl.ds(c, seq_count, stride=CHANNELS), :] = yintra[c] + result[:, at * LANES:(at + 1) * LANES]
        return 0

    lax.fori_loop(0, 4, across, 0)

    def gate(j, _):
        at = pl.ds(pl.multiple_of(j * CHANNELS, CHANNELS), CHANNELS)
        obuf[:, pl.ds(pl.multiple_of(j * LANES, LANES), LANES)] = (qfilt[at, :] * ybuf[at, :]).astype(BF16)
        return 0

    lax.fori_loop(0, seq_count, gate, 0, unroll=4)

    def sent_ids(n, _):
        ids_copy(n).wait_send()
        return 0

    lax.fori_loop(1, seq_count, sent_ids, 0)
    for copy in list(sib.values()) + list(cross.values()) + [energy1, energy2]:
        copy.wait_send()


def on_device(token_ids, embedding, norm_gain, projection, short_filter, residues, decay_rates):
    seq_count = lax.axis_size("seq")
    vocab, features = embedding.shape
    model_width = short_filter.shape[2]
    tokens = seq_count * LANES
    hbm = pl.BlockSpec(memory_space=pltpu.HBM)
    dma = pltpu.SemaphoreType.DMA
    vmem = pltpu.VMEM
    scratch = [
        vmem((vocab, features), BF16),
        vmem((features // LANES, LANES), F32),
        vmem((STREAMS, features, LANES), BF16),
        vmem((seq_count, 1, LANES), jnp.int32),
        vmem((STREAMS, TAPS, LANES), F32),
        vmem((MODES, LANES), F32),
        vmem((MODES, LANES), F32),
        vmem((STREAMS, features, 2 * LANES), BF16),
        vmem((STREAMS, 2, 2, CHANNELS, vocab), F32),
        vmem((STREAMS, 2, CHANNELS, vocab), F32),
        vmem((STREAMS, CHANNELS, vocab), F32),
        vmem((STREAMS, CHANNELS, vocab), F32),
        vmem((STREAMS, CHANNELS, vocab), F32),
        vmem((4, LANES), F32),
        vmem((4, LANES), F32),
        vmem((4, LANES), F32),
        vmem((4, LANES), F32),
        vmem((4, LANES), F32),
        vmem((4 * CHANNELS, HALF), BF16),
        vmem((2 * CHANNELS, HALF), BF16),
        vmem((seq_count, HALF, LANES), BF16),
        vmem((STREAMS * TAPS, CHANNELS, LANES), F32),
        vmem((CHANNELS, 2 * LANES, 2 * LANES), BF16),
        vmem((8, 2 * LANES, 4 * LANES), BF16),
        vmem((CHANNELS * MODES, LANES), F32),
        vmem((4, 8, LANES), F32),
        vmem((seq_count * CHANNELS, LANES), F32),
        vmem((seq_count * CHANNELS, LANES), F32),
        vmem((CHANNELS, seq_count, LANES), F32),
        vmem((4, seq_count, LANES), F32),
        vmem((4, seq_count, LANES), F32),
        vmem((seq_count * CHANNELS, LANES), F32),
        dma((12,)),
        dma((seq_count,)),
        dma((seq_count,)),
        dma((STREAMS,)),
        dma((STREAMS,)),
        dma((STREAMS,)),
        dma((STREAMS,)),
        dma((2,)),
        dma((2,)),
    ]
    return pl.pallas_call(
        functools.partial(kernel, model_width, seq_count),
        out_shape=vmem((CHANNELS, tokens), BF16),
        in_specs=[hbm] * 7,
        out_specs=pl.BlockSpec(memory_space=vmem),
        scratch_shapes=scratch,
        compiler_params=pltpu.CompilerParams(
            collective_id=0, has_side_effects=True, vmem_limit_bytes=56 * 1024 * 1024
        ),
    )(
        embedding,
        norm_gain.reshape(features // LANES, LANES),
        jnp.transpose(projection, (1, 0, 2)),
        token_ids.reshape(1, LANES),
        short_filter,
        jnp.transpose(residues),
        jnp.transpose(decay_rates),
    )


def solution(mesh):
    return jax.shard_map(
        on_device,
        mesh=mesh,
        in_specs=(P("seq"), P(None, "tp"), P("tp"), P("tp", None, "seq"), P(), P(), P()),
        out_specs=P(("seq", "tp"), None),
        check_vma=False,
    )
```

time: 1090 us -> 30 us (0.03)
  the two profiles are of different devices: /device:TPU:4 before, /device:TPU:1 now
where the time goes in v1:
time: 30 us; the launch traced here: 29.9 us
  Pallas kernels  29.1 us (97%)
  local copies, waits for them, and re-layouts  0.8 us (3%)
    pallas_call x1, Pallas kernels, on_device(): pl.pallas_call(functools.partial(kernel, model_width, seq_count), out_sha...  29.1 us
    unnamed x1, local copies, waits for them, and re-layouts  0.8 us

profile of v1, /device:TPU:1, one launch (start us, length us, event | category | flops | bytes accessed | tf_op | source)
XLA Modules:
  0.0 29.9 jit_solution(12478826122717408881)
XLA Ops:
  0.0 29.1 %shard_map.73 = bf16[32,8192]{1,0:T(8,128)(2,1)S(1)} custom-call(bf16[512,2048]{1,0:T(8,128)(2,1)} %emb_hbm.1, f32[16,128]{1,0:T(8,128)} %bitcast.8, bf16[3,2048,128]{2,1,0:T(8,128)(2,1)} %bitcast.5, s32[1,128]{1,0:T(1,128)} %bitcast.9, f32[3,3,8192]{2,1,0:T(4,128)} %filt_hbm.1, f32[16,8192]{1,0:T(8,128)} %bitcast.6, f32[16,8192]{1,0:T(8,128)} %bitcast.7), custom_call_target="tpu_custom_call" | custom-call | tf_op jit(solution)/shard_map/pallas_call | solution.py:458
  29.1 0.8 %copy.9 = bf16[32,8192]{1,0:T(8,128)(2,1)} copy(bf16[32,8192]{1,0:T(8,128)(2,1)S(1)} %shard_map.73) | data formatting | bytes 1048576

commit v2 on v1

--- a/solution.py
+++ b/solution.py
@@ -1,4 +1,5 @@
 import functools
+import math
 
 import jax
 import jax.numpy as jnp
@@ -57,17 +58,14 @@
     filt,
     res,
     rate,
+    column,
     wproj,
     part,
     recv1,
     own,
     send2,
     recv2,
-    en_part,
-    en_own,
-    en_recv1,
-    en_sum,
-    en_recv2,
+    en_all,
     tblkv,
     tblq,
     onehot,
@@ -91,6 +89,9 @@
     s2_recv,
     e_send,
     e_recv,
+    half_send,
+    half_recv,
+    here,
 ):
     seq = lax.axis_index("seq")
     tp = lax.axis_index("tp")
@@ -98,17 +99,43 @@
     far = tp // 2
     sibling = tp + 1 - 2 * core
     across_tp = lax.rem(tp + 2, 4)
+    diagonal = lax.rem(sibling + 2, 4)
+    peers_tp = (sibling, across_tp, diagonal)
+
+    plane = 2 * max(seq_count // 16, 1)
+    half = seq_count // 2
+
+    def at(m):
+        within = lax.rem(m, plane)
+        return (within // 2) * 16 + (m // plane) * 2 + lax.rem(within, 2)
+
+    def place_of(block):
+        return lax.rem(block // 2, 8) * plane + (block // 16) * 2 + lax.rem(block, 2)
+
+    me = place_of(seq)
+    early = me < half
+    known = jnp.where(early, half, seq_count)
+    first_greeted = jnp.where(early, 0, half)
+    partner = at(lax.rem(me + half, seq_count))
+
+    def each_other(first, last, act):
+        def one(m, _):
+            @pl.when(m != me)
+            def _():
+                act(m)
+
+            return 0
+
+        lax.fori_loop(first, last, one, 0)
 
     barrier = pltpu.get_barrier_semaphore()
-    for peer in (sibling, across_tp):
+
+    def greet(m):
+        pl.semaphore_signal(barrier, inc=1, device_id={"seq": at(m), "tp": tp}, device_id_type=MESH)
+
+    each_other(first_greeted, seq_count, greet)
+    for peer in peers_tp:
         pl.semaphore_signal(barrier, inc=1, device_id={"seq": seq, "tp": peer}, device_id_type=MESH)
-
-    def greet(n, _):
-        peer = lax.rem(seq + n, seq_count)
-        pl.semaphore_signal(barrier, inc=1, device_id={"seq": peer, "tp": tp}, device_id_type=MESH)
-        return 0
-
-    lax.fori_loop(1, seq_count, greet, 0)
 
     rows = emb_hbm.shape[0] // 4
     chan0 = pl.multiple_of(seq * LANES, LANES)
@@ -119,39 +146,55 @@
         loads[name].start()
 
     load("gain", 1, gain_hbm, gain)
-    load("proj1", 2, proj_hbm.at[1], proj.at[1])
+    for slot, name in enumerate(ORDER):
+        load(f"proj{name}", 2 + slot, proj_hbm.at[name], proj.at[name])
     for r in range(4):
-        load(f"emb{r}", 3 + r, emb_hbm.at[pl.ds(r * rows, rows), :], emb.at[pl.ds(r * rows, rows), :])
-    load("ids", 0, ids_hbm, ids.at[seq])
-    load("proj2", 7, proj_hbm.at[2], proj.at[2])
-    load("proj0", 8, proj_hbm.at[0], proj.at[0])
+        load(f"emb{r}", 5 + r, emb_hbm.at[pl.ds(r * rows, rows), :], emb.at[pl.ds(r * rows, rows), :])
+    load("ids", 0, ids_hbm, ids.at[me])
     load("rate", 9, rate_hbm.at[:, pl.ds(chan0, LANES)], rate)
     load("res", 10, res_hbm.at[:, pl.ds(chan0, LANES)], res)
     load("filt", 11, filt_hbm.at[:, :, pl.ds(chan0, LANES)], filt)
 
-    def ids_copy(n):
+    def ids_to(m):
         return pltpu.make_async_remote_copy(
-            src_ref=ids.at[seq], dst_ref=ids.at[seq],
-            send_sem=id_send.at[n], recv_sem=id_recv.at[n],
-            device_id={"seq": lax.rem(seq + n, seq_count), "tp": tp}, device_id_type=MESH,
-        )
-
-    def send_ids(n, _):
-        ids_copy(n).start()
-        return 0
-
-    def gained(s):
-        loads[f"proj{s}"].wait()
-
-        def one(k, _):
-            start = pl.multiple_of(k * LANES, LANES)
-            row = gain[pl.ds(k, 1), :]
-            column = jnp.transpose(jnp.broadcast_to(row, (LANES, LANES)))
-            hi, lo = split(proj[s, pl.ds(start, LANES), :].astype(F32) * column)
-            wproj[s, pl.ds(start, LANES), :] = jnp.concatenate([hi, lo], axis=1)
-            return 0
-
-        lax.fori_loop(0, proj.shape[1] // LANES, one, 0, unroll=2)
+            src_ref=ids.at[me], dst_ref=ids.at[me],
+            send_sem=id_send.at[m], recv_sem=id_recv.at[me],
+            device_id={"seq": at(m), "tp": tp}, device_id_type=MESH,
+        )
+
+    def ids_from(m):
+        return pltpu.make_async_remote_copy(
+            src_ref=ids.at[m], dst_ref=ids.at[m],
+            send_sem=id_send.at[m], recv_sem=id_recv.at[m],
+            device_id={"seq": at(m), "tp": tp}, device_id_type=MESH,
+        )
+
+    def first_half():
+        return pltpu.make_async_remote_copy(
+            src_ref=ids.at[pl.ds(0, half)], dst_ref=ids.at[pl.ds(0, half)],
+            send_sem=half_send, recv_sem=half_recv,
+            device_id={"seq": partner, "tp": tp}, device_id_type=MESH,
+        )
+
+    def gained():
+        features = proj.shape[1]
+        loads["gain"].wait()
+        gain_rows = gain.shape[0]
+        turned = jnp.transpose(
+            jnp.concatenate([gain[...], jnp.zeros((LANES - gain_rows, LANES), F32)], axis=0)
+        )
+        for k in range(gain_rows):
+            column[k * LANES:(k + 1) * LANES, :] = jnp.broadcast_to(turned[:, k:k + 1], (LANES, LANES))
+        for s in ORDER:
+            loads[f"proj{s}"].wait()
+
+            def one(k, _):
+                span = pl.ds(pl.multiple_of(k * LANES, LANES), LANES)
+                hi, lo = split(proj[s, span, :].astype(F32) * column[span, :])
+                wproj[s, span, :] = jnp.concatenate([hi, lo], axis=1)
+                return 0
+
+            lax.fori_loop(0, features // LANES, one, 0, unroll=math.gcd(4, features // LANES))
 
     def project(s, first):
         for r in range(4):
@@ -192,111 +235,141 @@
             for k in range(emb.shape[1] // LANES):
                 piece = block[:, k * LANES:(k + 1) * LANES].astype(F32)
                 total = total + piece * piece
-            en_part[pl.ds(r, 1), :] = jnp.sum(jnp.transpose(total), axis=0, keepdims=True)
-
-    def send_energy(step, src, dst, peer):
-        copy = pltpu.make_async_remote_copy(
-            src_ref=src, dst_ref=dst, send_sem=e_send.at[step], recv_sem=e_recv.at[step],
+            en_all[tp, pl.ds(r, 1), :] = jnp.sum(jnp.transpose(total), axis=0, keepdims=True)
+
+    def energy_to(peer):
+        return pltpu.make_async_remote_copy(
+            src_ref=en_all.at[tp], dst_ref=en_all.at[tp], send_sem=e_send.at[peer], recv_sem=e_recv.at[tp],
             device_id={"seq": seq, "tp": peer}, device_id_type=MESH,
         )
-        copy.start()
-        return copy
-
-    loads["gain"].wait()
-    gained(1)
+
+    def energy_from(peer):
+        return pltpu.make_async_remote_copy(
+            src_ref=en_all.at[peer], dst_ref=en_all.at[peer], send_sem=e_send.at[peer], recv_sem=e_recv.at[peer],
+            device_id={"seq": seq, "tp": peer}, device_id_type=MESH,
+        )
+
+    def enter():
+        loads["ids"].wait()
+        pl.semaphore_wait(barrier, known + 2)
+
+        @pl.when(jnp.logical_not(early))
+        def _():
+            pl.semaphore_signal(here, inc=1, device_id={"seq": partner, "tp": tp}, device_id_type=MESH)
+
+        each_other(0, known, lambda m: ids_to(m).start())
+
+    def prepare():
+        loads["rate"].wait()
+        loads["res"].wait()
+        loads["filt"].wait()
+        turn = lax.rem(LANES - tp * CHANNELS, LANES)
+        rates = pltpu.roll(rate[...], turn, 1)
+        twice = 2.0 * rates
+        series = twice * (
+            1.0 - twice / 2 * (1.0 - twice / 3 * (1.0 - twice / 4 * (1.0 - twice / 5 * (1.0 - twice / 6))))
+        )
+        lost = jnp.where(twice < 0.125, series, 1.0 - jnp.exp(-twice))
+        mode = pltpu.roll(res[...], turn, 1) * jnp.sqrt(lost)
+        lane16 = lax.broadcasted_iota(jnp.int32, (MODES, LANES), 1).astype(F32)
+        lquad[...] = jnp.zeros(lquad.shape, BF16)
+        for c in range(CHANNELS):
+            rate_c = jnp.broadcast_to(rates[:, c:c + 1], (MODES, LANES))
+            mode_c = jnp.broadcast_to(mode[:, c:c + 1], (MODES, LANES))
+            hi, lo = split(mode_c * jnp.exp(-rate_c * (lane16 + 1.0)))
+            colw[pl.ds(c * MODES, MODES), :] = rate_c
+            quad, at = c // 4, c % 4
+            cols = pl.ds(at * LANES, LANES)
+            lquad[quad, pl.ds(at * MODES, MODES), cols] = hi
+            lquad[quad, pl.ds(64 + at * MODES, MODES), cols] = hi
+            lquad[quad, pl.ds(128 + 64 * (quad % 2) + at * MODES, MODES), cols] = lo
+        row_at = lax.broadcasted_iota(jnp.int32, (LANES, LANES), 0)
+        lane_at = lax.broadcasted_iota(jnp.int32, (LANES, LANES), 1)
+        behind = (LANES - 1 - row_at).astype(F32)
+        keep = lane_at >= row_at
+
+        def operators(g, _):
+            start = pl.multiple_of(g * LANES, LANES)
+            rate_row = jnp.transpose(colw[pl.ds(start, LANES), :])
+            step_rate[g] = rate_row[:8, :] * LANES
+            decays = jnp.exp(-rate_row * behind)
+            e_hi, e_lo = split(decays)
+            grown = quad_operands(jnp.exp(rate_row * (row_at + 1).astype(F32)))
+            for half in range(2):
+                kernels = jnp.dot(grown[half], lquad[g * 2 + half], preferred_element_type=F32)
+                for at in range(4):
+                    inner = jnp.where(keep, kernels[:, at * LANES:(at + 1) * LANES], 0.0)
+                    t_hi, t_lo = split(inner)
+                    c_in = half * 4 + at
+                    mine = (lane_at >= c_in * MODES) & (lane_at < (c_in + 1) * MODES)
+                    zero = jnp.zeros((LANES, LANES), F32)
+                    m_hi = jnp.where(mine, e_hi.astype(F32), zero).astype(BF16)
+                    m_lo = jnp.where(mine, e_lo.astype(F32), zero).astype(BF16)
+                    c = g * 8 + c_in
+                    weights[c, pl.ds(0, LANES), :] = jnp.concatenate([t_hi, m_hi], axis=1)
+                    weights[c, pl.ds(LANES, LANES), :] = jnp.concatenate([t_lo, m_lo], axis=1)
+            return 0
+
+        lax.fori_loop(0, 4, operators, 0)
+
+        for s in range(STREAMS):
+            moved = pltpu.roll(filt[s], turn, 1)
+            columns = jnp.transpose(jnp.concatenate([moved, jnp.zeros((LANES - TAPS, LANES), F32)], axis=0))
+            for j in range(TAPS):
+                taps[s * TAPS + j] = jnp.broadcast_to(columns[:CHANNELS, j:j + 1], (CHANNELS, LANES))
+
+    gained()
     project(1, True)
-    gained(2)
-    project(2, False)
-    loads["ids"].wait()
-
-    pl.semaphore_wait(barrier, seq_count + 1)
-    lax.fori_loop(1, seq_count, send_ids, 0)
-    sib = {1: send_sibling(1), 2: send_sibling(2)}
+
+    @pl.when(early)
+    def _():
+        project(2, False)
+        project(0, False)
+
+    enter()
+    sib = {1: send_sibling(1)}
+
+    @pl.when(jnp.logical_not(early))
+    def _():
+        project(2, False)
+
+    sib[2] = send_sibling(2)
+    cross = {1: send_across(1, sib[1])}
+
+    @pl.when(jnp.logical_not(early))
+    def _():
+        project(0, False)
+
+    sib[0] = send_sibling(0)
+    cross[2] = send_across(2, sib[2])
+
     energies()
-    energy1 = send_energy(0, en_part, en_recv1, sibling)
-    cross = {1: send_across(1, sib[1]), 2: send_across(2, sib[2])}
-    gained(0)
-    project(0, False)
-    sib[0] = send_sibling(0)
-    energy1.wait_recv()
-    en_sum[...] = en_part[...] + en_recv1[...]
-    energy2 = send_energy(1, en_sum, en_recv2, across_tp)
+    for peer in peers_tp:
+        energy_to(peer).start()
     cross[0] = send_across(0, sib[0])
-
-    loads["rate"].wait()
-    loads["res"].wait()
-    loads["filt"].wait()
-    turn = lax.rem(LANES - tp * CHANNELS, LANES)
-    rates = pltpu.roll(rate[...], turn, 1)
-    twice = 2.0 * rates
-    series = twice * (
-        1.0 - twice / 2 * (1.0 - twice / 3 * (1.0 - twice / 4 * (1.0 - twice / 5 * (1.0 - twice / 6))))
-    )
-    lost = jnp.where(twice < 0.125, series, 1.0 - jnp.exp(-twice))
-    mode = pltpu.roll(res[...], turn, 1) * jnp.sqrt(lost)
-    lane16 = lax.broadcasted_iota(jnp.int32, (MODES, LANES), 1).astype(F32)
-    lquad[...] = jnp.zeros(lquad.shape, BF16)
-    for c in range(CHANNELS):
-        rate_c = jnp.broadcast_to(rates[:, c:c + 1], (MODES, LANES))
-        mode_c = jnp.broadcast_to(mode[:, c:c + 1], (MODES, LANES))
-        hi, lo = split(mode_c * jnp.exp(-rate_c * (lane16 + 1.0)))
-        colw[pl.ds(c * MODES, MODES), :] = rate_c
-        quad, at = c // 4, c % 4
-        cols = pl.ds(at * LANES, LANES)
-        lquad[quad, pl.ds(at * MODES, MODES), cols] = hi
-        lquad[quad, pl.ds(64 + at * MODES, MODES), cols] = hi
-        lquad[quad, pl.ds(128 + 64 * (quad % 2) + at * MODES, MODES), cols] = lo
-    row_at = lax.broadcasted_iota(jnp.int32, (LANES, LANES), 0)
-    lane_at = lax.broadcasted_iota(jnp.int32, (LANES, LANES), 1)
-    behind = (LANES - 1 - row_at).astype(F32)
-    keep = lane_at >= row_at
-
-    def operators(g, _):
-        start = pl.multiple_of(g * LANES, LANES)
-        rate_row = jnp.transpose(colw[pl.ds(start, LANES), :])
-        step_rate[g] = rate_row[:8, :] * LANES
-        decays = jnp.exp(-rate_row * behind)
-        e_hi, e_lo = split(decays)
-        grown = quad_operands(jnp.exp(rate_row * (row_at + 1).astype(F32)))
-        for half in range(2):
-            kernels = jnp.dot(grown[half], lquad[g * 2 + half], preferred_element_type=F32)
-            for at in range(4):
-                inner = jnp.where(keep, kernels[:, at * LANES:(at + 1) * LANES], 0.0)
-                t_hi, t_lo = split(inner)
-                c_in = half * 4 + at
-                mine = (lane_at >= c_in * MODES) & (lane_at < (c_in + 1) * MODES)
-                zero = jnp.zeros((LANES, LANES), F32)
-                m_hi = jnp.where(mine, e_hi.astype(F32), zero).astype(BF16)
-                m_lo = jnp.where(mine, e_lo.astype(F32), zero).astype(BF16)
-                c = g * 8 + c_in
-                weights[c, pl.ds(0, LANES), :] = jnp.concatenate([t_hi, m_hi], axis=1)
-                weights[c, pl.ds(LANES, LANES), :] = jnp.concatenate([t_lo, m_lo], axis=1)
-        return 0
-
-    lax.fori_loop(0, 4, operators, 0)
-
-    for s in range(STREAMS):
-        moved = pltpu.roll(filt[s], turn, 1)
-        columns = jnp.transpose(jnp.concatenate([moved, jnp.zeros((LANES - TAPS, LANES), F32)], axis=0))
-        for j in range(TAPS):
-            taps[s * TAPS + j] = jnp.broadcast_to(columns[:CHANNELS, j:j + 1], (CHANNELS, LANES))
+    prepare()
 
     row_of = lax.broadcasted_iota(jnp.int32, (HALF, LANES), 0)
 
-    def mark(slot):
-        low = jnp.broadcast_to(ids[slot] & (HALF - 1), (HALF, LANES))
-        onehot[slot] = jnp.where(row_of == low, 1.0, 0.0).astype(BF16)
-
-    def arrive(n, _):
-        ids_copy(n).wait_recv()
-        mark(lax.rem(seq + seq_count - n, seq_count))
-        return 0
-
-    mark(seq)
-    lax.fori_loop(1, seq_count, arrive, 0)
-
-    energy2.wait_recv()
-    scale = lax.rsqrt((en_sum[...] + en_recv2[...]) / model_width + 1e-05)
+    def mark(m):
+        low = jnp.broadcast_to(ids[m] & (HALF - 1), (HALF, LANES))
+        onehot[at(m)] = jnp.where(row_of == low, 1.0, 0.0).astype(BF16)
+
+    def arrive(m):
+        ids_from(m).wait_recv()
+        mark(m)
+
+    mark(me)
+
+    @pl.when(early)
+    def _():
+        each_other(0, half, arrive)
+        pl.semaphore_wait(here, 1)
+        first_half().start()
+
+    for peer in peers_tp:
+        energy_from(peer).wait_recv()
+    scale = lax.rsqrt((en_all[0] + en_all[1] + en_all[2] + en_all[3]) / model_width + 1e-05)
 
     def tabulate(s, place, table):
         cross[s].wait_recv()
@@ -306,6 +379,20 @@
             value = (own[s, :, lanes] + recv2[s, :, lanes]) * scale[q:q + 1, :]
             table[pl.ds((q // 2) * height + place * CHANNELS, CHANNELS), pl.ds((q % 2) * LANES, LANES)] = value.astype(BF16)
 
+    tabulate(1, 0, tblkv)
+    tabulate(2, 1, tblkv)
+    each_other(half, seq_count, arrive)
+
+    @pl.when(jnp.logical_not(early))
+    def _():
+        first_half().wait_recv()
+
+        def one(m, _):
+            mark(m)
+            return 0
+
+        lax.fori_loop(0, half, one, 0)
+
     def filter_streams(table, streams, unroll, emit):
         height = table.shape[0] // 2
         lane = lax.broadcasted_iota(jnp.int32, (height, LANES), 1)
@@ -318,7 +405,7 @@
             both = jnp.dot(table[...], hot, preferred_element_type=F32)
             for u in range(2):
                 j = 2 * i + u
-                upper = jnp.broadcast_to(ids[j], (height, LANES)) >= HALF
+                upper = jnp.broadcast_to(ids[place_of(j)], (height, LANES)) >= HALF
                 lanes = slice(u * LANES, (u + 1) * LANES)
                 now = jnp.where(upper, both[height:, lanes], both[:height, lanes])
                 one, two = pltpu.roll(now, 1, 1), pltpu.roll(now, 2, 1)
@@ -343,8 +430,6 @@
     def emit_query(at, q):
         qfilt[at, :] = q
 
-    tabulate(1, 0, tblkv)
-    tabulate(2, 1, tblkv)
     filter_streams(tblkv, (1, 2), 8, emit_gated)
     tabulate(0, 0, tblq)
     filter_streams(tblq, (0,), 8, emit_query)
@@ -395,12 +480,9 @@
 
     lax.fori_loop(0, seq_count, gate, 0, unroll=4)
 
-    def sent_ids(n, _):
-        ids_copy(n).wait_send()
-        return 0
-
-    lax.fori_loop(1, seq_count, sent_ids, 0)
-    for copy in list(sib.values()) + list(cross.values()) + [energy1, energy2]:
+    each_other(0, known, lambda m: ids_to(m).wait_send())
+    pl.when(early)(first_half().wait_send)
+    for copy in list(sib.values()) + list(cross.values()) + [energy_to(peer) for peer in peers_tp]:
         copy.wait_send()
 
 
@@ -420,17 +502,14 @@
         vmem((STREAMS, TAPS, LANES), F32),
         vmem((MODES, LANES), F32),
         vmem((MODES, LANES), F32),
+        vmem((features, LANES), F32),
         vmem((STREAMS, features, 2 * LANES), BF16),
         vmem((STREAMS, 2, 2, CHANNELS, vocab), F32),
         vmem((STREAMS, 2, CHANNELS, vocab), F32),
         vmem((STREAMS, CHANNELS, vocab), F32),
         vmem((STREAMS, CHANNELS, vocab), F32),
         vmem((STREAMS, CHANNELS, vocab), F32),
-        vmem((4, LANES), F32),
-        vmem((4, LANES), F32),
-        vmem((4, LANES), F32),
-        vmem((4, LANES), F32),
-        vmem((4, LANES), F32),
+        vmem((4, 4, LANES), F32),
         vmem((4 * CHANNELS, HALF), BF16),
         vmem((2 * CHANNELS, HALF), BF16),
         vmem((seq_count, HALF, LANES), BF16),
@@ -452,8 +531,11 @@
         dma((STREAMS,)),
         dma((STREAMS,)),
         dma((STREAMS,)),
-        dma((2,)),
-        dma((2,)),
+        dma((4,)),
+        dma((4,)),
+        dma(()),
+        dma(()),
+        pltpu.SemaphoreType.REGULAR,
     ]
     return pl.pallas_call(
         functools.partial(kernel, model_width, seq_count),

time: 30 us -> 28.5 us (0.950)
  Pallas kernels: 29.1 us -> 27.5 us
    pallas_call x1, Pallas kernels: 29.1 us -> 27.5 us  [on_device(): pl.pallas_call(functools.partial(kernel, model_width, seq_count), out_sha...]
where the time goes in v2:
time: 28.5 us; the launch traced here: 28.3 us
  Pallas kernels  27.5 us (96%)
  local copies, waits for them, and re-layouts  0.8 us (3%)
    pallas_call x1, Pallas kernels, on_device(): pl.pallas_call(functools.partial(kernel, model_width, seq_count), out_sha...  27.5 us
    unnamed x1, local copies, waits for them, and re-layouts  0.8 us

profile of v2, /device:TPU:1, one launch (start us, length us, event | category | flops | bytes accessed | tf_op | source)
XLA Modules:
  0.0 28.3 jit_solution(8646727253791691368)
XLA Ops:
  0.0 27.5 %shard_map.73 = bf16[32,8192]{1,0:T(8,128)(2,1)S(1)} custom-call(bf16[512,2048]{1,0:T(8,128)(2,1)} %emb_hbm.1, f32[16,128]{1,0:T(8,128)} %bitcast.8, bf16[3,2048,128]{2,1,0:T(8,128)(2,1)} %bitcast.5, s32[1,128]{1,0:T(1,128)} %bitcast.9, f32[3,3,8192]{2,1,0:T(4,128)} %filt_hbm.1, f32[16,8192]{1,0:T(8,128)} %bitcast.6, f32[16,8192]{1,0:T(8,128)} %bitcast.7), custom_call_target="tpu_custom_call" | custom-call | tf_op jit(solution)/shard_map/pallas_call | solution.py:540
  27.6 0.8 %copy.9 = bf16[32,8192]{1,0:T(8,128)(2,1)} copy(bf16[32,8192]{1,0:T(8,128)(2,1)S(1)} %shard_map.73) | data formatting | bytes 1048576

commit v3 on v2

--- a/solution.py
+++ b/solution.py
@@ -89,8 +89,8 @@
     s2_recv,
     e_send,
     e_recv,
-    half_send,
-    half_recv,
+    piece_send,
+    piece_recv,
     here,
 ):
     seq = lax.axis_index("seq")
@@ -113,10 +113,15 @@
         return lax.rem(block // 2, 8) * plane + (block // 16) * 2 + lax.rem(block, 2)
 
     me = place_of(seq)
+    quarter = seq_count // 4
+    first = me < quarter
     early = me < half
-    known = jnp.where(early, half, seq_count)
-    first_greeted = jnp.where(early, 0, half)
-    partner = at(lax.rem(me + half, seq_count))
+    second = jnp.logical_and(early, jnp.logical_not(first))
+    late = jnp.logical_not(early)
+    known = jnp.where(first, quarter, jnp.where(early, half, seq_count))
+    first_greeted = jnp.where(first, 0, jnp.where(early, quarter, half))
+    near_partner = at(lax.rem(me + jnp.where(first, quarter, seq_count - quarter), seq_count))
+    far_partner = at(lax.rem(me + half, seq_count))
 
     def each_other(first, last, act):
         def one(m, _):
@@ -169,12 +174,15 @@
             device_id={"seq": at(m), "tp": tp}, device_id_type=MESH,
         )
 
-    def first_half():
+    def in_one_piece(amount, slot, peer):
         return pltpu.make_async_remote_copy(
-            src_ref=ids.at[pl.ds(0, half)], dst_ref=ids.at[pl.ds(0, half)],
-            send_sem=half_send, recv_sem=half_recv,
-            device_id={"seq": partner, "tp": tp}, device_id_type=MESH,
-        )
+            src_ref=ids.at[pl.ds(0, amount)], dst_ref=ids.at[pl.ds(0, amount)],
+            send_sem=piece_send.at[slot], recv_sem=piece_recv.at[slot],
+            device_id={"seq": peer, "tp": tp}, device_id_type=MESH,
+        )
+
+    first_quarter = in_one_piece(quarter, 0, near_partner)
+    first_half = in_one_piece(half, 1, far_partner)
 
     def gained():
         features = proj.shape[1]
@@ -253,10 +261,15 @@
         loads["ids"].wait()
         pl.semaphore_wait(barrier, known + 2)
 
-        @pl.when(jnp.logical_not(early))
+        @pl.when(second)
         def _():
-            pl.semaphore_signal(here, inc=1, device_id={"seq": partner, "tp": tp}, device_id_type=MESH)
-
+            pl.semaphore_signal(here.at[0], inc=1, device_id={"seq": near_partner, "tp": tp}, device_id_type=MESH)
+
+        @pl.when(late)
+        def _():
+            pl.semaphore_signal(here.at[1], inc=1, device_id={"seq": far_partner, "tp": tp}, device_id_type=MESH)
+
+    def send_ids():
         each_other(0, known, lambda m: ids_to(m).start())
 
     def prepare():
@@ -320,33 +333,15 @@
 
     gained()
     project(1, True)
-
-    @pl.when(early)
-    def _():
-        project(2, False)
-        project(0, False)
-
+    project(2, False)
+    project(0, False)
     enter()
-    sib = {1: send_sibling(1)}
-
-    @pl.when(jnp.logical_not(early))
-    def _():
-        project(2, False)
-
-    sib[2] = send_sibling(2)
-    cross = {1: send_across(1, sib[1])}
-
-    @pl.when(jnp.logical_not(early))
-    def _():
-        project(0, False)
-
-    sib[0] = send_sibling(0)
-    cross[2] = send_across(2, sib[2])
-
+    sib = {s: send_sibling(s) for s in ORDER}
+    send_ids()
+    cross = {s: send_across(s, sib[s]) for s in ORDER}
     energies()
     for peer in peers_tp:
         energy_to(peer).start()
-    cross[0] = send_across(0, sib[0])
     prepare()
 
     row_of = lax.broadcasted_iota(jnp.int32, (HALF, LANES), 0)
@@ -359,13 +354,34 @@
         ids_from(m).wait_recv()
         mark(m)
 
+    def mark_all(amount):
+        def one(m, _):
+            mark(m)
+            return 0
+
+        lax.fori_loop(0, amount, one, 0)
+
     mark(me)
+
+    @pl.when(first)
+    def _():
+        each_other(0, quarter, arrive)
+        pl.semaphore_wait(here.at[0], 1)
+        first_quarter.start()
 
     @pl.when(early)
     def _():
-        each_other(0, half, arrive)
-        pl.semaphore_wait(here, 1)
-        first_half().start()
+        each_other(quarter, half, arrive)
+
+    @pl.when(second)
+    def _():
+        first_quarter.wait_recv()
+        mark_all(quarter)
+
+    @pl.when(early)
+    def _():
+        pl.semaphore_wait(here.at[1], 1)
+        first_half.start()
 
     for peer in peers_tp:
         energy_from(peer).wait_recv()
@@ -383,17 +399,12 @@
     tabulate(2, 1, tblkv)
     each_other(half, seq_count, arrive)
 
-    @pl.when(jnp.logical_not(early))
+    @pl.when(late)
     def _():
-        first_half().wait_recv()
-
-        def one(m, _):
-            mark(m)
-            return 0
-
-        lax.fori_loop(0, half, one, 0)
-
-    def filter_streams(table, streams, unroll, emit):
+        first_half.wait_recv()
+        mark_all(half)
+
+    def filter_streams(table, streams, emit):
         height = table.shape[0] // 2
         lane = lax.broadcasted_iota(jnp.int32, (height, LANES), 1)
         first_lane = lane < 1
@@ -422,7 +433,7 @@
             return before1, before2
 
         nothing = jnp.zeros((height, LANES), F32)
-        lax.fori_loop(0, seq_count // 2, pair, (nothing, nothing), unroll=unroll)
+        lax.fori_loop(0, seq_count // 2, pair, (nothing, nothing), unroll=seq_count // 2)
 
     def emit_gated(at, k, v):
         gated[at, :] = (k * v).astype(BF16).astype(F32)
@@ -430,9 +441,9 @@
     def emit_query(at, q):
         qfilt[at, :] = q
 
-    filter_streams(tblkv, (1, 2), 8, emit_gated)
+    filter_streams(tblkv, (1, 2), emit_gated)
     tabulate(0, 0, tblq)
-    filter_streams(tblq, (0,), 8, emit_query)
+    filter_streams(tblq, (0,), emit_query)
 
     def inside(g, _):
         total = jnp.zeros((seq_count, LANES), F32)
@@ -445,7 +456,7 @@
         ends[g] = total
         return 0
 
-    lax.fori_loop(0, 4, inside, 0)
+    lax.fori_loop(0, 4, inside, 0, unroll=4)
 
     sub = lax.broadcasted_iota(jnp.int32, (8, LANES), 0)
     for g in range(4):
@@ -471,17 +482,18 @@
                 ybuf[pl.ds(c, seq_count, stride=CHANNELS), :] = yintra[c] + result[:, at * LANES:(at + 1) * LANES]
         return 0
 
-    lax.fori_loop(0, 4, across, 0)
+    lax.fori_loop(0, 4, across, 0, unroll=4)
 
     def gate(j, _):
         at = pl.ds(pl.multiple_of(j * CHANNELS, CHANNELS), CHANNELS)
         obuf[:, pl.ds(pl.multiple_of(j * LANES, LANES), LANES)] = (qfilt[at, :] * ybuf[at, :]).astype(BF16)
         return 0
 
-    lax.fori_loop(0, seq_count, gate, 0, unroll=4)
+    lax.fori_loop(0, seq_count, gate, 0, unroll=8)
 
     each_other(0, known, lambda m: ids_to(m).wait_send())
-    pl.when(early)(first_half().wait_send)
+    pl.when(first)(first_quarter.wait_send)
+    pl.when(early)(first_half.wait_send)
     for copy in list(sib.values()) + list(cross.values()) + [energy_to(peer) for peer in peers_tp]:
         copy.wait_send()
 
@@ -533,9 +545,9 @@
         dma((STREAMS,)),
         dma((4,)),
         dma((4,)),
-        dma(()),
-        dma(()),
-        pltpu.SemaphoreType.REGULAR,
+        dma((2,)),
+        dma((2,)),
+        pltpu.SemaphoreType.REGULAR((2,)),
     ]
     return pl.pallas_call(
         functools.partial(kernel, model_width, seq_count),

time: 28.5 us -> 25.6 us (0.90)
  Pallas kernels: 27.5 us -> 24.7 us
    pallas_call x1, Pallas kernels: 27.5 us -> 24.7 us  [on_device(): pl.pallas_call(functools.partial(kernel, model_width, seq_count), out_sha...]
where the time goes in v3:
time: 25.6 us; the launch traced here: 25.5 us
  Pallas kernels  24.7 us (96%)
  local copies, waits for them, and re-layouts  0.8 us (3%)
    pallas_call x1, Pallas kernels, on_device(): pl.pallas_call(functools.partial(kernel, model_width, seq_count), out_sha...  24.7 us
    unnamed x1, local copies, waits for them, and re-layouts  0.8 us

profile of v3, /device:TPU:1, one launch (start us, length us, event | category | flops | bytes accessed | tf_op | source)
XLA Modules:
  0.0 25.5 jit_solution(16437493443264007318)
XLA Ops:
  0.0 24.7 %shard_map.73 = bf16[32,8192]{1,0:T(8,128)(2,1)S(1)} custom-call(bf16[512,2048]{1,0:T(8,128)(2,1)} %emb_hbm.1, f32[16,128]{1,0:T(8,128)} %bitcast.8, bf16[3,2048,128]{2,1,0:T(8,128)(2,1)} %bitcast.5, s32[1,128]{1,0:T(1,128)} %bitcast.9, f32[3,3,8192]{2,1,0:T(4,128)} %filt_hbm.1, f32[16,8192]{1,0:T(8,128)} %bitcast.6, f32[16,8192]{1,0:T(8,128)} %bitcast.7), custom_call_target="tpu_custom_call" | custom-call | tf_op jit(solution)/shard_map/pallas_call | solution.py:552
  24.7 0.8 %copy.9 = bf16[32,8192]{1,0:T(8,128)(2,1)} copy(bf16[32,8192]{1,0:T(8,128)(2,1)S(1)} %shard_map.73) | data formatting | bytes 1048576

commit v4 on v3

--- a/solution.py
+++ b/solution.py
@@ -120,8 +120,8 @@
     late = jnp.logical_not(early)
     known = jnp.where(first, quarter, jnp.where(early, half, seq_count))
     first_greeted = jnp.where(first, 0, jnp.where(early, quarter, half))
-    near_partner = at(lax.rem(me + jnp.where(first, quarter, seq_count - quarter), seq_count))
-    far_partner = at(lax.rem(me + half, seq_count))
+    group = me // quarter
+    leader = at(lax.rem(me, quarter))
 
     def each_other(first, last, act):
         def one(m, _):
@@ -132,15 +132,6 @@
             return 0
 
         lax.fori_loop(first, last, one, 0)
-
-    barrier = pltpu.get_barrier_semaphore()
-
-    def greet(m):
-        pl.semaphore_signal(barrier, inc=1, device_id={"seq": at(m), "tp": tp}, device_id_type=MESH)
-
-    each_other(first_greeted, seq_count, greet)
-    for peer in peers_tp:
-        pl.semaphore_signal(barrier, inc=1, device_id={"seq": seq, "tp": peer}, device_id_type=MESH)
 
     rows = emb_hbm.shape[0] // 4
     chan0 = pl.multiple_of(seq * LANES, LANES)
@@ -160,6 +151,15 @@
     load("res", 10, res_hbm.at[:, pl.ds(chan0, LANES)], res)
     load("filt", 11, filt_hbm.at[:, :, pl.ds(chan0, LANES)], filt)
 
+    barrier = pltpu.get_barrier_semaphore()
+
+    def greet(m):
+        pl.semaphore_signal(barrier, inc=1, device_id={"seq": at(m), "tp": tp}, device_id_type=MESH)
+
+    for peer in peers_tp:
+        pl.semaphore_signal(barrier, inc=1, device_id={"seq": seq, "tp": peer}, device_id_type=MESH)
+    each_other(first_greeted, seq_count, greet)
+
     def ids_to(m):
         return pltpu.make_async_remote_copy(
             src_ref=ids.at[me], dst_ref=ids.at[me],
@@ -181,8 +181,8 @@
             device_id={"seq": peer, "tp": tp}, device_id_type=MESH,
         )
 
-    first_quarter = in_one_piece(quarter, 0, near_partner)
-    first_half = in_one_piece(half, 1, far_partner)
+    def piece_to(later):
+        return in_one_piece(quarter if later == 1 else half, later, at(lax.rem(me, quarter) + later * quarter))
 
     def gained():
         features = proj.shape[1]
@@ -261,13 +261,9 @@
         loads["ids"].wait()
         pl.semaphore_wait(barrier, known + 2)
 
-        @pl.when(second)
+        @pl.when(jnp.logical_not(first))
         def _():
-            pl.semaphore_signal(here.at[0], inc=1, device_id={"seq": near_partner, "tp": tp}, device_id_type=MESH)
-
-        @pl.when(late)
-        def _():
-            pl.semaphore_signal(here.at[1], inc=1, device_id={"seq": far_partner, "tp": tp}, device_id_type=MESH)
+            pl.semaphore_signal(here.at[group], inc=1, device_id={"seq": leader, "tp": tp}, device_id_type=MESH)
 
     def send_ids():
         each_other(0, known, lambda m: ids_to(m).start())
@@ -343,6 +339,9 @@
     for peer in peers_tp:
         energy_to(peer).start()
     prepare()
+    each_other(0, known, lambda m: ids_to(m).wait_send())
+    for copy in list(sib.values()) + [energy_to(peer) for peer in peers_tp]:
+        copy.wait_send()
 
     row_of = lax.broadcasted_iota(jnp.int32, (HALF, LANES), 0)
 
@@ -366,22 +365,23 @@
     @pl.when(first)
     def _():
         each_other(0, quarter, arrive)
-        pl.semaphore_wait(here.at[0], 1)
-        first_quarter.start()
+        pl.semaphore_wait(here.at[1], 1)
+        piece_to(1).start()
 
     @pl.when(early)
     def _():
         each_other(quarter, half, arrive)
 
+    @pl.when(first)
+    def _():
+        for later in (2, 3):
+            pl.semaphore_wait(here.at[later], 1)
+            piece_to(later).start()
+
     @pl.when(second)
     def _():
-        first_quarter.wait_recv()
+        in_one_piece(quarter, 1, leader).wait_recv()
         mark_all(quarter)
-
-    @pl.when(early)
-    def _():
-        pl.semaphore_wait(here.at[1], 1)
-        first_half.start()
 
     for peer in peers_tp:
         energy_from(peer).wait_recv()
@@ -401,7 +401,7 @@
 
     @pl.when(late)
     def _():
-        first_half.wait_recv()
+        in_one_piece(half, group, leader).wait_recv()
         mark_all(half)
 
     def filter_streams(table, streams, emit):
@@ -491,10 +491,13 @@
 
     lax.fori_loop(0, seq_count, gate, 0, unroll=8)
 
-    each_other(0, known, lambda m: ids_to(m).wait_send())
-    pl.when(first)(first_quarter.wait_send)
-    pl.when(early)(first_half.wait_send)
-    for copy in list(sib.values()) + list(cross.values()) + [energy_to(peer) for peer in peers_tp]:
+
+    @pl.when(first)
+    def _():
+        for later in (1, 2, 3):
+            piece_to(later).wait_send()
+
+    for copy in cross.values():
         copy.wait_send()
 
 
@@ -545,9 +548,9 @@
         dma((STREAMS,)),
         dma((4,)),
         dma((4,)),
-        dma((2,)),
-        dma((2,)),
-        pltpu.SemaphoreType.REGULAR((2,)),
+        dma((4,)),
+        dma((4,)),
+        pltpu.SemaphoreType.REGULAR((4,)),
     ]
     return pl.pallas_call(
         functools.partial(kernel, model_width, seq_count),

time: 25.6 us -> 25 us (0.977)
  Pallas kernels: 24.7 us -> 24.1 us
    pallas_call x1, Pallas kernels: 24.7 us -> 24.1 us  [on_device(): pl.pallas_call(functools.partial(kernel, model_width, seq_count), out_sha...]
where the time goes in v4:
time: 25 us; the launch traced here: 24.9 us
  Pallas kernels  24.1 us (96%)
  local copies, waits for them, and re-layouts  0.8 us (3%)
    pallas_call x1, Pallas kernels, on_device(): pl.pallas_call(functools.partial(kernel, model_width, seq_count), out_sha...  24.1 us
    unnamed x1, local copies, waits for them, and re-layouts  0.8 us

profile of v4, /device:TPU:1, one launch (start us, length us, event | category | flops | bytes accessed | tf_op | source)
XLA Modules:
  0.0 24.9 jit_solution(6834960762822756702)
XLA Ops:
  0.0 24.1 %shard_map.73 = bf16[32,8192]{1,0:T(8,128)(2,1)S(1)} custom-call(bf16[512,2048]{1,0:T(8,128)(2,1)} %emb_hbm.1, f32[16,128]{1,0:T(8,128)} %bitcast.8, bf16[3,2048,128]{2,1,0:T(8,128)(2,1)} %bitcast.5, s32[1,128]{1,0:T(1,128)} %bitcast.9, f32[3,3,8192]{2,1,0:T(4,128)} %filt_hbm.1, f32[16,8192]{1,0:T(8,128)} %bitcast.6, f32[16,8192]{1,0:T(8,128)} %bitcast.7), custom_call_target="tpu_custom_call" | custom-call | tf_op jit(solution)/shard_map/pallas_call | solution.py:555
  24.1 0.8 %copy.9 = bf16[32,8192]{1,0:T(8,128)(2,1)} copy(bf16[32,8192]{1,0:T(8,128)(2,1)S(1)} %shard_map.73) | data formatting | bytes 1048576

commit v5 on v4

--- a/solution.py
+++ b/solution.py
@@ -330,11 +330,14 @@
     gained()
     project(1, True)
     project(2, False)
+    enter()
+    sib = {1: send_sibling(1), 2: send_sibling(2)}
+    send_ids()
+    cross = {1: send_across(1, sib[1])}
     project(0, False)
-    enter()
-    sib = {s: send_sibling(s) for s in ORDER}
-    send_ids()
-    cross = {s: send_across(s, sib[s]) for s in ORDER}
+    sib[0] = send_sibling(0)
+    cross[2] = send_across(2, sib[2])
+    cross[0] = send_across(0, sib[0])
     energies()
     for peer in peers_tp:
         energy_to(peer).start()

time: 25 us -> 24.5 us (0.980)
  Pallas kernels: 24.1 us -> 23.6 us
    pallas_call x1, Pallas kernels: 24.1 us -> 23.6 us  [on_device(): pl.pallas_call(functools.partial(kernel, model_width, seq_count), out_sha...]
where the time goes in v5:
time: 24.5 us; the launch traced here: 24.4 us
  Pallas kernels  23.6 us (96%)
  local copies, waits for them, and re-layouts  0.8 us (3%)
    pallas_call x1, Pallas kernels, on_device(): pl.pallas_call(functools.partial(kernel, model_width, seq_count), out_sha...  23.6 us
    unnamed x1, local copies, waits for them, and re-layouts  0.8 us

profile of v5, /device:TPU:1, one launch (start us, length us, event | category | flops | bytes accessed | tf_op | source)
XLA Modules:
  0.0 24.4 jit_solution(10503559210362681035)
XLA Ops:
  0.0 23.6 %shard_map.73 = bf16[32,8192]{1,0:T(8,128)(2,1)S(1)} custom-call(bf16[512,2048]{1,0:T(8,128)(2,1)} %emb_hbm.1, f32[16,128]{1,0:T(8,128)} %bitcast.8, bf16[3,2048,128]{2,1,0:T(8,128)(2,1)} %bitcast.5, s32[1,128]{1,0:T(1,128)} %bitcast.9, f32[3,3,8192]{2,1,0:T(4,128)} %filt_hbm.1, f32[16,8192]{1,0:T(8,128)} %bitcast.6, f32[16,8192]{1,0:T(8,128)} %bitcast.7), custom_call_target="tpu_custom_call" | custom-call | tf_op jit(solution)/shard_map/pallas_call | solution.py:558
  23.6 0.8 %copy.9 = bf16[32,8192]{1,0:T(8,128)(2,1)} copy(bf16[32,8192]{1,0:T(8,128)(2,1)S(1)} %shard_map.73) | data formatting | bytes 1048576

commit v6 on v5

--- a/solution.py
+++ b/solution.py
@@ -536,12 +536,12 @@
         vmem((8, 2 * LANES, 4 * LANES), BF16),
         vmem((CHANNELS * MODES, LANES), F32),
         vmem((4, 8, LANES), F32),
-        vmem((seq_count * CHANNELS, LANES), F32),
-        vmem((seq_count * CHANNELS, LANES), F32),
+        vmem(((seq_count + 1) * CHANNELS, LANES), F32),
+        vmem(((seq_count + 1) * CHANNELS, LANES), F32),
         vmem((CHANNELS, seq_count, LANES), F32),
         vmem((4, seq_count, LANES), F32),
         vmem((4, seq_count, LANES), F32),
-        vmem((seq_count * CHANNELS, LANES), F32),
+        vmem(((seq_count + 1) * CHANNELS, LANES), F32),
         dma((12,)),
         dma((seq_count,)),
         dma((seq_count,)),

time: 24.5 us -> 24.5 us (level)
  no operation moved by 1% of the time
where the time goes in v6:
time: 24.5 us; the launch traced here: 24.4 us
  Pallas kernels  23.6 us (96%)
  local copies, waits for them, and re-layouts  0.8 us (3%)
    pallas_call x1, Pallas kernels, on_device(): pl.pallas_call(functools.partial(kernel, model_width, seq_count), out_sha...  23.6 us
    unnamed x1, local copies, waits for them, and re-layouts  0.8 us

profile of v6, /device:TPU:1, one launch (start us, length us, event | category | flops | bytes accessed | tf_op | source)
XLA Modules:
  0.0 24.4 jit_solution(14935291245404567113)
XLA Ops:
  0.0 23.6 %shard_map.73 = bf16[32,8192]{1,0:T(8,128)(2,1)S(1)} custom-call(bf16[512,2048]{1,0:T(8,128)(2,1)} %emb_hbm.1, f32[16,128]{1,0:T(8,128)} %bitcast.8, bf16[3,2048,128]{2,1,0:T(8,128)(2,1)} %bitcast.5, s32[1,128]{1,0:T(1,128)} %bitcast.9, f32[3,3,8192]{2,1,0:T(4,128)} %filt_hbm.1, f32[16,8192]{1,0:T(8,128)} %bitcast.6, f32[16,8192]{1,0:T(8,128)} %bitcast.7), custom_call_target="tpu_custom_call" | custom-call | tf_op jit(solution)/shard_map/pallas_call | solution.py:558
  23.6 0.8 %copy.9 = bf16[32,8192]{1,0:T(8,128)(2,1)} copy(bf16[32,8192]{1,0:T(8,128)(2,1)S(1)} %shard_map.73) | data formatting | bytes 1048576
